TPU v7x, 32 devices: a whole 2x2x4 slice. The times are simulated.
32 devices in a mesh: groups: 2 (over x), row: 16 (over z, y, core), col: 1.
Axes of the slice: x: 2, y: 2, z: 4, core: 2. Of those that a mesh axis runs over, the one named last changes fastest.
Arguments:
- tokens: bfloat16 [512, 5120], P(('groups', 'row')), parts along dimension 0, may hold values from -6 to 6
- hidden_gradient: bfloat16 [512, 24576], P('groups', ('row', 'col')), parts along dimension 0, may hold values from -6 to 6
- gate_projection_weight: bfloat16 [24576, 5120], P(('row', 'col')), may hold values from -0.078125 to 0.078125
- up_projection_weight: bfloat16 [24576, 5120], P(('row', 'col')), may hold values from -0.078125 to 0.078125
- adapter_down_maps: bfloat16 [32, 5120, 16], P(('groups', 'row', 'col')), parts along dimension 0, may hold values from -0.078125 to 0.078125
- adapter_up_maps: bfloat16 [32, 16, 24576], P(('groups', 'row', 'col')), parts along dimension 0, may hold values from -1.5 to 1.5
- padded_block_tenant: int32 [4], P('groups'), parts along dimension 0, may hold values from 0 to 15
- tenant_adapter_slot: int32 [32], P('groups'), parts along dimension 0, may hold values from 0 to 15, each once
- block_live_count: int32 [4], P('groups'), parts along dimension 0, may hold values from 1 to 128, 192 in all
Outputs:
- input_gradient: bfloat16 [512, 5120], P(('groups', 'row', 'col')), parts along dimension 0
- down_grad: bfloat16 [32, 5120, 16], P(('groups', 'row', 'col')), parts along dimension 0
- up_grad: bfloat16 [32, 16, 24576], P(('groups', 'row', 'col')), parts along dimension 0
There are 2 independent parts, one for each index of `groups`. A program takes and returns all parts, laid end to end along the dimension named above; an argument that names none is the same for every part. Nothing has to cross between parts.
All inputs are finite; a program needn't handle non-finite values.
Results may differ from a plain program's by a relative error of at most 0.006.
Values may be sent and summed in bfloat16 or wider, within the bound.
A program may use at most 192 MiB of HBM per device.

v0:
```python
import jax
import jax.numpy as jnp
from jax import lax
from jax.sharding import PartitionSpec as P

BLOCK = 128


ADAPTER_SCALE = 0.5


def body(
    tokens,
    hidden_gradient,
    gate_projection_weight,
    up_projection_weight,
    adapter_down_maps,
    adapter_up_maps,
    padded_block_tenant,
    tenant_adapter_slot,
    block_live_count,
):
    own_index = lax.axis_index(("row", "col"))
    tenants_per_device = adapter_down_maps.shape[0]
    tenants = tenant_adapter_slot.shape[0]
    shard_width = gate_projection_weight.shape[0]
    panel = lax.all_gather(tokens, "row", axis=0, tiled=True)
    tok_total = panel.shape[0]
    model_width = panel.shape[1]
    num_blocks = tok_total // BLOCK
    tenant_ids = jnp.arange(tenants, dtype=jnp.int32)
    block_adapter_slot = jnp.sum(
        jnp.where(
            padded_block_tenant[:, None] == tenant_ids[None, :], tenant_adapter_slot[None, :], 0
        ),
        axis=1,
    )
    block_owner = block_adapter_slot // tenants_per_device
    local_slot = block_adapter_slot % tenants_per_device
    local_selection = (
        (block_owner == own_index)[:, None]
        & (local_slot[:, None] == jnp.arange(tenants_per_device, dtype=jnp.int32)[None, :])
    ).astype(jnp.bfloat16)
    all_pick = (block_adapter_slot[:, None] == tenant_ids[None, :]).astype(jnp.bfloat16)
    down_own = jnp.einsum(
        "pz,zfq->pfq", local_selection, adapter_down_maps, preferred_element_type=jnp.float32
    ).astype(jnp.bfloat16)
    blocks = panel.reshape(num_blocks, BLOCK, model_width)
    code_part = jnp.einsum("bid,bdr->bir", blocks, down_own, preferred_element_type=jnp.float32)
    latent_rows = lax.psum(code_part, ("row", "col")).astype(jnp.bfloat16)
    token_segments = lax.all_to_all(
        adapter_up_maps, ("row", "col"), split_axis=2, concat_axis=0, tiled=True
    )
    adapter_up = jnp.einsum(
        "bp,prf->brf", all_pick, token_segments, preferred_element_type=jnp.float32
    ).astype(jnp.bfloat16)
    adapter_gate_term = jnp.einsum(
        "lme,leq->lmq", latent_rows, adapter_up, preferred_element_type=jnp.float32
    ).reshape(tok_total, shard_width)
    gate_activation = (
        jnp.einsum("td,fd->tf", panel, gate_projection_weight, preferred_element_type=jnp.float32)
        + ADAPTER_SCALE * adapter_gate_term
    )
    up_act = jnp.einsum(
        "td,fd->tf", panel, up_projection_weight, preferred_element_type=jnp.float32
    )
    live_rows = (
        (jnp.arange(BLOCK, dtype=jnp.int32)[None, :] < block_live_count[:, None])
        .reshape(tok_total)
        .astype(jnp.float32)
    )
    sigmoid_gate = jax.nn.sigmoid(gate_activation)
    masked_grad = hidden_gradient.astype(jnp.float32) * live_rows[:, None]
    dgate = (
        masked_grad * up_act * sigmoid_gate * (1.0 + gate_activation * (1.0 - sigmoid_gate))
    ).astype(jnp.bfloat16)
    dup = (masked_grad * gate_activation * sigmoid_gate).astype(jnp.bfloat16)
    gate_gradient_blocks = dgate.reshape(num_blocks, BLOCK, shard_width)
    grad_part = jnp.einsum(
        "bif,brf->bir", gate_gradient_blocks, adapter_up, preferred_element_type=jnp.float32
    )
    latent_gradient = lax.psum(grad_part, ("row", "col")).astype(jnp.bfloat16)
    adapter_input_term = ADAPTER_SCALE * jnp.einsum(
        "tqy,tly->tql", latent_gradient, down_own, preferred_element_type=jnp.float32
    ).reshape(tok_total, model_width)
    primary_rows = jnp.dot(dgate, gate_projection_weight, preferred_element_type=jnp.float32)
    primary_rows = primary_rows + jnp.dot(
        dup, up_projection_weight, preferred_element_type=jnp.float32
    )
    summed = lax.psum_scatter(
        primary_rows + adapter_input_term, ("row", "col"), scatter_dimension=0, tiled=True
    )
    input_gradient = summed.astype(jnp.bfloat16)
    blockwise_down_maps = ADAPTER_SCALE * jnp.einsum(
        "qes,qen->qsn", blocks, latent_gradient, preferred_element_type=jnp.float32
    )
    down_grad = jnp.einsum(
        "bs,bdr->sdr",
        local_selection.astype(jnp.float32),
        blockwise_down_maps,
        precision=lax.Precision.HIGHEST,
    ).astype(jnp.bfloat16)
    blockwise_up_maps = ADAPTER_SCALE * jnp.einsum(
        "zde,zdk->zek", latent_rows, gate_gradient_blocks, preferred_element_type=jnp.float32
    )
    slot_part = jnp.einsum(
        "bp,brf->prf",
        all_pick.astype(jnp.float32),
        blockwise_up_maps,
        precision=lax.Precision.HIGHEST,
    )
    arrived = lax.all_to_all(
        slot_part.astype(jnp.bfloat16), ("row", "col"), split_axis=0, concat_axis=2, tiled=True
    ).astype(slot_part.dtype)
    up_grad = arrived.astype(jnp.bfloat16)
    return (input_gradient, down_grad, up_grad)


def solution(mesh):
    return jax.shard_map(
        body,
        mesh=mesh,
        in_specs=(
            P(("groups", "row"), None),
            P("groups", ("row", "col")),
            P(("row", "col"), None),
            P(("row", "col"), None),
            P(("groups", "row", "col"), None, None),
            P(("groups", "row", "col"), None, None),
            P("groups"),
            P("groups"),
            P("groups"),
        ),
        out_specs=(
            P(("groups", "row", "col"), None),
            P(("groups", "row", "col"), None, None),
            P(("groups", "row", "col"), None, None),
        ),
        check_vma=False,
    )
```

profile of v0, /device:TPU:0, one launch (start us, length us, event | category | flops | bytes accessed | tf_op | source)
XLA Modules:
  0.0 493.1 jit_solution(2457215043619707380)
XLA Ops:
  7.2 0.7 all-gather.2.cloned.1.call-update
  7.9 22.8 %copy.26 = bf16[1,16,24576]{1,0,2:T(2,128)(2,1)} copy(bf16[1,16,24576]{2,1,0:T(8,128)(2,1)} %param.14) | data formatting | bytes 1572864 | tf_op args[5]
  30.7 0.5 broadcast.95
  31.2 134.9 %reduce = bf16[24576,16]{1,0:T(8,128)(2,1)} reduce(bf16[24576,1,16]{2,1,0:T(2,128)(2,1)} %bitcast.63, bf16[]{:T(256)} %broadcast.95), dimensions={1}, to_apply=%bitcast.43.reduce_sub_computation | reduce | bytes 1572866
  166.1 9.7 %reshape.58 = bf16[16,2,12288]{2,1,0:T(2,128)(2,1)} reshape(bf16[24576,16]{1,0:T(8,128)(2,1)} %reduce) | data formatting | bytes 1572864
  175.8 7.4 %all-to-all-start = ((bf16[16,2,12288]{2,1,0:T(2,128)(2,1)}), bf16[16,2,12288]{2,1,0:T(2,128)(2,1)S(1)}, u32[]{:S(2)}, u32[]{:S(2)}) async-start(bf16[16,2,12288]{2,1,0:T(2,128)(2,1)} %reshape.58), calls=%async_computation | async-start | bytes 1572864 | tf_op jit(solution)/shard_map/all_to_all | solution.py:51
  183.6 18.3 %all-to-all-done = bf16[16,2,12288]{2,1,0:T(2,128)(2,1)S(1)} async-done(((bf16[16,2,12288]{2,1,0:T(2,128)(2,1)}), bf16[16,2,12288]{2,1,0:T(2,128)(2,1)S(1)}, u32[]{:S(2)}, u32[]{:S(2)}) %all-to-all-start) | async-done | bytes 786464 | tf_op jit(solution)/shard_map/all_to_all | solution.py:51
  201.9 12.0 %reshape.59 = bf16[24576,1,16]{2,1,0:T(2,128)(2,1)} reshape(bf16[16,2,12288]{2,1,0:T(2,128)(2,1)S(1)} %all-to-all-done) | data formatting | bytes 1572864
  213.9 22.6 %copy.27 = bf16[1,16,24576]{2,1,0:T(8,128)(2,1)S(1)} copy(bf16[1,16,24576]{1,0,2:T(2,128)(2,1)} %bitcast.62) | data formatting | bytes 1572864 | tf_op jit(solution)/shard_map/all_to_all | solution.py:51
  236.5 0.2 copy.36
  236.7 0.3 convolution_convert_fusion.1
  237.1 2.7 convolution_bitcast_fusion
  239.8 61.5 %psum.14 = bf16[2,128,16]{1,2,0:T(8,128)(2,1)S(1)} all-reduce(f32[2,128,16]{1,2,0:T(8,128)S(1)} %convolution_bitcast_fusion), channel_id=1, replica_groups=mesh['groups'=2,'row'=16,'col'=1] {'row','col'}, use_global_device_ids=true, to_apply=%region_1.2 | all-reduce | flops 4096 | bytes 24576 | tf_op jit(solution)/shard_map/psum | solution.py:50
  301.3 1.6 convolution_multiply_fusion.2
  302.9 9.5 %convolution_add_fusion.1 = f32[256,1536]{1,0:T(8,128)} fusion(f32[256,1536]{1,0:T(8,128)} %bitcast.72, bf16[256,5120]{1,0:T(8,128)(2,1)S(1)} %copy-done, bf16[1536,5120]{1,0:T(8,128)(2,1)} %param.11), kind=kOutput, calls=%fused_computation.9 | convolution fusion | flops 4026925056 | bytes 21495808 | tf_op jit(solution)/shard_map/td,fd->tf/dot_general | solution.py:61
  312.5 10.7 %fusion.4 = bf16[256,1536]{1,0:T(8,128)(2,1)S(1)} fusion(bf16[256,5120]{1,0:T(8,128)(2,1)S(1)} %copy-done, bf16[1536,5120]{1,0:T(8,128)(2,1)} %param.12, f32[256,1536]{1,0:T(8,128)} %convolution_add_fusion.1, bf16[256,1536]{1,0:T(8,128)(2,1)} %param.10, f32[256]{0:T(256)S(1)} %fusion.26), kind=kOutput, calls=%fused_computation.10 | convolution fusion | flops 4031250432 | bytes 21496832 | tf_op jit(solution)/shard_map/td,fd->tf/dot_general | solution.py:64
  323.2 11.4 %fusion.32 = f32[256,5120]{1,0:T(8,128)} fusion(bf16[256,1536]{1,0:T(8,128)(2,1)S(1)} %fusion.4, bf16[1536,5120]{1,0:T(8,128)(2,1)} %param.11), kind=kOutput, calls=%fused_computation.53 | convolution fusion | flops 4026531840 | bytes 21757952 | tf_op jit(solution)/shard_map/dot_general | solution.py:86
  334.6 0.3 fusion.15
  334.9 57.8 %psum.15 = bf16[2,128,16]{1,2,0:T(8,128)(2,1)S(1)} all-reduce(f32[2,128,16]{1,2,0:T(8,128)S(1)} %fusion.15), channel_id=1, replica_groups=mesh['groups'=2,'row'=16,'col'=1] {'row','col'}, use_global_device_ids=true, to_apply=%region_2.3 | all-reduce | flops 4096 | bytes 24576 | tf_op jit(solution)/shard_map/psum | solution.py:82
  392.8 2.0 convolution_multiply_fusion
  394.8 0.6 copy-done.1
  395.3 13.4 %fusion = f32[256,5120]{1,0:T(8,128)} fusion(f32[256,5120]{1,0:T(8,128)S(1)} %bitcast.64, f32[256,5120]{1,0:T(8,128)S(1)} %copy-done.1, bf16[1536,5120]{1,0:T(8,128)(2,1)} %param.12, f32[256,1536]{1,0:T(8,128)} %convolution_add_fusion.1, bf16[256,1536]{1,0:T(8,128)(2,1)} %param.10, f32[256]{0:T(256)S(1)} %fusion.26), kind=kOutput, calls=%fused_computation.2 | convolution fusion | flops 4032299008 | bytes 33817600 | tf_op jit(solution)/shard_map/dot_general | solution.py:87
  409.0 1.0 convolution_convert_fusion
  409.9 1.3 copy.31
  411.2 3.9 all-to-all-start.1
  415.1 0.5 fusion.1
  415.6 35.5 %fusion.7 = bf16[1,5120,16]{0,1,2:T(8,128)(2,1)} fusion(f32[2,5120,16]{1,2,0:T(8,128)S(1)} %fusion.1, s32[2]{0:T(128)S(1)} %fusion.27, s32[]{:T(128)S(6)} %axis_index.16), kind=kOutput, calls=%fused_computation.21 | convolution fusion | flops 1966082 | bytes 819212 | tf_op jit(solution)/shard_map/bs,bdr->sdr/dot_general | solution.py:97
  451.1 15.5 %copy.34 = bf16[1,5120,16]{1,2,0:T(8,128)(2,1)S(1)} copy(bf16[1,5120,16]{0,1,2:T(8,128)(2,1)} %fusion.7) | data formatting | bytes 327680 | tf_op jit(solution)/shard_map/bs,bdr->sdr/dot_general | solution.py:97
  466.6 0.7 fusion.14
  467.3 0.9 copy.35
  468.2 16.3 %reduce-scatter.2.cloned.1.call-done = f32[16,5120]{1,0:T(8,128)} async-done(((f32[256,5120]{1,0:T(8,128)}), f32[16,5120]{1,0:T(8,128)}) %reduce-scatter.2.cloned.1.call-update) | async-done | bytes 327696 | tf_op jit(solution)/shard_map/reduce_scatter | solution.py:90
  484.6 1.7 convert_element_type.58
  (23 shorter events, 0.6 us)
Async XLA Ops:
  7.2 229.9 %all-gather.2.cloned.1.call-start = ((), (), s32[]{:S(2)}) async-start(), calls=%async_computation.3 | async-start | bytes 2785280 | tf_op jit(solution)/shard_map/all_gather | solution.py:27
  166.1 17.1 %copy-start.4 = (s32[16]{0:T(128)S(1)}, s32[16]{0:T(128)}, u32[]{:S(2)}) copy-start(s32[16]{0:T(128)} %param.16) | copy-start | bytes 196
  166.1 17.1 %copy-start.5 = (s32[2]{0:T(128)S(1)}, s32[2]{0:T(128)}, u32[]{:S(2)}) copy-start(s32[2]{0:T(128)} %param.15) | copy-start | bytes 28
  166.1 17.3 %copy-start.6 = (s32[2]{0:T(128)S(1)}, s32[2]{0:T(128)}, u32[]{:S(2)}) copy-start(s32[2]{0:T(128)} %param.17) | copy-start | bytes 28
  166.1 17.4 %copy-start.3 = (bf16[1,5120,16]{1,2,0:T(8,128)(2,1)S(1)}, bf16[1,5120,16]{1,2,0:T(8,128)(2,1)}, u32[]{:S(2)}) copy-start(bf16[1,5120,16]{1,2,0:T(8,128)(2,1)} %param.13) | copy-start | bytes 491524
  175.8 26.1 %all-to-all-start = ((bf16[16,2,12288]{2,1,0:T(2,128)(2,1)}), bf16[16,2,12288]{2,1,0:T(2,128)(2,1)S(1)}, u32[]{:S(2)}, u32[]{:S(2)}) async-start(bf16[16,2,12288]{2,1,0:T(2,128)(2,1)} %reshape.58), calls=%async_computation | async-start | bytes 1572864 | tf_op jit(solution)/shard_map/all_to_all | solution.py:51
  183.2 301.4 %reduce-scatter.2.cloned.1.call-start = ((), (), s32[]{:S(2)}) async-start(), calls=%async_computation.4 | async-start | bytes 5570560 | tf_op jit(solution)/shard_map/reduce_scatter | solution.py:90
  183.6 53.5 %copy-start.2 = (f32[5120,16]{0,1:T(8,128)}, f32[5120,16]{0,1:T(8,128)S(1)}, u32[]{:S(2)}) copy-start(f32[5120,16]{0,1:T(8,128)S(1)} %bitcast_convert_fusion.1) | copy-start | bytes 983044
  237.1 65.8 %copy-start = (bf16[256,5120]{1,0:T(8,128)(2,1)S(1)}, bf16[256,5120]{1,0:T(8,128)(2,1)}, u32[]{:S(2)}) copy-start(bf16[256,5120]{1,0:T(8,128)(2,1)} %all-gather.2.cloned.1.call-done) | copy-start | bytes 7864324
  392.8 2.6 copy-start.1
  411.2 56.1 %all-to-all-start.1 = ((bf16[16,16,1536]{2,1,0:T(8,128)(2,1)}), bf16[16,16,1536]{2,1,0:T(8,128)(2,1)S(1)}, u32[]{:S(2)}, u32[]{:S(2)}) async-start(bf16[16,16,1536]{2,1,0:T(8,128)(2,1)} %copy.31), calls=%async_computation.2 | async-start | bytes 1572864 | tf_op jit(solution)/shard_map/all_to_all | solution.py:112
Sparse Core Ops, SparseCore 0:
  10.3 45.9 all-gather.1
  408.9 75.6 reduce-scatter.1
where the time goes:
time: 497 us; the launch traced here: 493 us
  other arithmetic  137 us (28%)
  blocking collectives  119 us (24%)
  matrix products  89.1 us (18%)
  local copies, waits for them, and re-layouts  86.8 us (17%)
  waiting for transfers between devices  35.4 us (7%)
  between operations  14.2 us (3%)
  starting transfers between devices  11.3 us (2%)
    unnamed x1, other arithmetic  135 us
    psum x1, blocking collectives, body(): latent_rows = lax.psum(code_part, ('row', 'col')).astype(jnp.bfloat16)  61.5 us
    psum x1, blocking collectives, body(): latent_gradient = lax.psum(grad_part, ('row', 'col')).astype(jnp.bfloat16)  57.8 us
    unnamed x19, local copies, waits for them, and re-layouts  45.8 us
    dot_general x1, matrix products, body(): jnp.einsum('bs,bdr->sdr', local_selection.astype(jnp.float32), blockwise_...  35.5 us
    all_to_all x1, local copies, waits for them, and re-layouts, body(): lax.all_to_all(adapter_up_maps, ('row', 'col'), split_axis=2, concat_axis...  22.6 us
    all_to_all x1, waiting for transfers between devices, body(): lax.all_to_all(adapter_up_maps, ('row', 'col'), split_axis=2, concat_axis...  18.3 us
    reduce_scatter x1, waiting for transfers between devices, body(): lax.psum_scatter(primary_rows + adapter_input_term, ('row', 'col'), scatt...  16.3 us
  transfers between devices with their start and end apart: 4, of which 2 were waited for; matrix products, arithmetic and copies ran while one was open for 53% of the time, Pallas kernels for 0%

commit v1 on v0

v1 whole, which is shorter than its diff:
```python
import functools

import jax
import jax.numpy as jnp
from jax import lax
from jax.experimental import pallas as pl
from jax.experimental.pallas import tpu as pltpu
from jax.sharding import PartitionSpec as P

BLOCK = 128
ADAPTER_SCALE = 0.5
CHUNKS = 4
BF16 = jnp.bfloat16
F32 = jnp.float32


def dot(a, b, ca, cb):
    return lax.dot_general(a, b, (((ca,), (cb,)), ((), ())), preferred_element_type=F32)


def each(lo, hi, body):
    def step(i, carry):
        body(i)
        return carry

    lax.fori_loop(lo, hi, step, 0)


def kernel(
    dims,
    tok_in, hid_ref, gate_hbm, up_hbm, down_ref, maps_ref, tenant_ref, slot_ref, live_ref,
    din_ref, ddown_ref, dmaps_ref,
    wg, wu, tok, acc_g, acc_u, dgate, dup, part,
    cs_buf, cr_buf, ys_buf, yr_buf, zs_buf, zr_buf,
    mcs_buf, mcr_buf, mys_buf, myr_buf, mzs_buf, mzr_buf, maps,
    codes_buf, cgrad_buf, ugrad_buf,
    w_sem, tz_sem, ty_sem, tc_sem, uz_sem, uy_sem, uc_sem,
    rc_sem, ry_sem, rz_sem, mc_sem, my_sem, mz_sem, code_sem, cgrad_sem,
):
    nz, ny, ncol = dims
    n = nz * ny * 2
    rows, width = tok_in.shape
    total = n * rows
    blocks = total // BLOCK
    hidden = wg.shape[0]
    rank = down_ref.shape[0]
    cw = width // CHUNKS
    me = lax.axis_index("row") * ncol + lax.axis_index("col")
    z, y, c = me // (2 * ny), (me // 2) % ny, me % 2

    def index(zz, yy, cc):
        return (zz * ny + yy) * 2 + cc

    def device(i):
        return {"row": i // ncol, "col": i % ncol}

    def remote(src, dst, sems, target):
        return pltpu.make_async_remote_copy(
            src_ref=src,
            dst_ref=dst,
            send_sem=sems[0],
            recv_sem=sems[1],
            device_id=device(target),
            device_id_type=pl.DeviceIdType.MESH,
        )

    y_peer, c_peer = index(z, ny - 1 - y, c), index(z, y, 1 - c)

    def weight_copy(k, which):
        src, dst = ((gate_hbm, wg), (up_hbm, wu))[which]
        cols = pl.ds(k * cw, cw)
        return pltpu.make_async_copy(src.at[:, cols], dst.at[:, cols], w_sem.at[k, which])

    for k in range(CHUNKS):
        for which in range(2):
            weight_copy(k, which).start()

    barrier = pltpu.get_barrier_semaphore()

    def greet(d):
        pl.semaphore_signal(
            barrier, inc=1, device_id=device((me + d) % n), device_id_type=pl.DeviceIdType.MESH
        )

    each(1, n, greet)
    tok[me] = tok_in[...]
    pl.semaphore_wait(barrier, n - 1)

    class Gather:
        def __init__(self, view, zsem, ysem, csem, k):
            self.view, self.k = view, k
            self.zsem, self.ysem, self.csem = zsem, ysem, csem

        def z_copy(self, d, shard):
            sems = (self.zsem.at[0, self.k, d], self.zsem.at[1, self.k, d])
            v = self.view(shard)
            return remote(v, v, sems, index((z + d) % nz, y, c))

        def y_copy(self, d, shard):
            sems = (self.ysem.at[0, self.k, d], self.ysem.at[1, self.k, d])
            v = self.view(shard)
            return remote(v, v, sems, y_peer)

        def c_copy(self, j, shard):
            sems = (self.csem.at[0, self.k, j], self.csem.at[1, self.k, j])
            v = self.view(shard)
            return remote(v, v, sems, c_peer)

        def start(self):
            each(1, nz, lambda d: self.z_copy(d, me).start())
            if ny > 1:
                self.y_copy(0, me).start()
            self.c_copy(0, me).start()

        def on_z(self):
            def arrived(d):
                shard = index((z + nz - d) % nz, y, c)
                self.z_copy(d, shard).wait_recv()
                if ny > 1:
                    self.y_copy(d, shard).start()
                self.c_copy(d, shard).start()

            each(1, nz, arrived)

        def on_y(self):
            def arrived(d):
                shard = index((z + nz - d) % nz, ny - 1 - y, c)
                self.y_copy(d, shard).wait_recv()
                self.c_copy(nz + d, shard).start()

            if ny > 1:
                each(0, nz, arrived)

        def on_c(self):
            each(0, nz * ny, lambda j: self.c_copy(j, me).wait_recv())

        def finish(self):
            each(1, nz, lambda d: self.z_copy(d, me).wait_send())
            if ny > 1:
                each(0, nz, lambda d: self.y_copy(d, me).wait_send())
            each(0, nz * ny, lambda j: self.c_copy(j, me).wait_send())

    class Reduce:
        def __init__(self, piece, bufs, sems, k):
            self.piece, self.k = piece, k
            self.cs, self.cr, self.ys, self.yr, self.zs, self.zr = [b.at[k] for b in bufs]
            csem, ysem, zsem = sems
            self.c_copy = remote(self.cs, self.cr, (csem.at[0, k], csem.at[1, k]), c_peer)
            self.y_copy = remote(self.ys, self.yr, (ysem.at[0, k], ysem.at[1, k]), y_peer)
            self.zsem = zsem

        def z_copy(self, d):
            sems = (self.zsem.at[0, self.k, d], self.zsem.at[1, self.k, d])
            return remote(self.zs.at[d], self.zr.at[d], sems, index((z + d) % nz, y, c))

        def start(self):
            def fill(j):
                self.cs[j] = self.piece(j * 2 + 1 - c).astype(BF16)

            each(0, nz * ny, fill)
            self.c_copy.start()

        def chip_sum(self, zz, yy):
            return self.piece(index(zz, yy, c)) + self.cr[zz * ny + yy].astype(F32)

        def on_c(self):
            self.c_copy.wait_recv()

            def fill(zz):
                self.ys[zz] = self.chip_sum(zz, ny - 1 - y).astype(BF16)

            if ny > 1:
                each(0, nz, fill)
                self.y_copy.start()

        def y_sum(self, zz):
            value = self.chip_sum(zz, y)
            if ny > 1:
                value = value + self.yr[zz].astype(F32)
            return value

        def on_y(self):
            if ny > 1:
                self.y_copy.wait_recv()

            def send(d):
                self.zs[d] = self.y_sum((z + d) % nz).astype(BF16)
                self.z_copy(d).start()

            each(1, nz, send)

        def result(self):
            def add(d, value):
                self.z_copy(d).wait_recv()
                return value + self.zr[d].astype(F32)

            return lax.fori_loop(1, nz, add, self.y_sum(z))

        def finish(self):
            self.c_copy.wait_send()
            if ny > 1:
                self.y_copy.wait_send()
            each(1, nz, lambda d: self.z_copy(d).wait_send())

    def to_all(buf, sem):
        def copy(d, shard):
            return remote(buf.at[shard], buf.at[shard], (sem.at[0, d], sem.at[1, d]), (me + d) % n)

        return (
            lambda: each(1, n, lambda d: copy(d, me).start()),
            lambda: each(1, n, lambda d: copy(d, (me + n - d) % n).wait_recv()),
            lambda: each(1, n, lambda d: copy(d, me).wait_send()),
        )

    slots = [slot_ref[tenant_ref[b]] for b in range(blocks)]
    chosen = [jnp.where(s == me, 1.0, 0.0).astype(F32) for s in slots]
    token_block = lax.broadcasted_iota(jnp.int32, (1, total), 1) // BLOCK
    token_chosen = jnp.zeros((1, total), F32)
    for b in range(blocks):
        token_chosen = jnp.where(token_block == b, chosen[b], token_chosen)

    def map_piece(i):
        cols = pl.ds(pl.multiple_of(i * hidden, 128), hidden)
        one = maps_ref[:, cols].astype(F32)
        return jnp.concatenate([one * chosen[b] for b in range(blocks)], axis=0)

    map_reduce = Reduce(
        map_piece,
        (mcs_buf, mcr_buf, mys_buf, myr_buf, mzs_buf, mzr_buf),
        (mc_sem, my_sem, mz_sem),
        0,
    )
    gathers = [
        Gather(
            lambda shard, k=k: tok.at[shard, :, pl.ds(k * cw, cw)], tz_sem, ty_sem, tc_sem, k
        )
        for k in range(CHUNKS)
    ]

    for g in gathers:
        g.start()
    map_reduce.start()

    tile = min(hidden, 512)
    half = min(hidden, 256) if hidden % 256 == 0 else 128

    def token_chunk(k):
        return tok[:, :, k * cw:(k + 1) * cw].reshape(total, cw)

    def forward(k):
        weight_copy(k, 0).wait()
        weight_copy(k, 1).wait()
        tk = token_chunk(k)

        def step(t):
            span = pl.ds(pl.multiple_of(t * tile, 128), tile)
            g = dot(tk, wg[span, k * cw:(k + 1) * cw], 1, 1)
            u = dot(tk, wu[span, k * cw:(k + 1) * cw], 1, 1)
            if k == 0:
                acc_g[:, span] = g
                acc_u[:, span] = u
            else:
                acc_g[:, span] += g
                acc_u[:, span] += u

        each(0, hidden // tile, step)

    own_codes = jnp.zeros((rank, total), F32)
    for i in range(CHUNKS + 2):
        if i < CHUNKS:
            gathers[i].on_z()
        if i == CHUNKS - 1:
            map_reduce.on_c()
        if 0 <= i - 1 < CHUNKS:
            gathers[i - 1].on_y()
        if i == CHUNKS:
            map_reduce.on_y()
        if i >= 2:
            k = i - 2
            gathers[k].on_c()
            own_codes = own_codes + dot(
                down_ref[:, k * cw:(k + 1) * cw], token_chunk(k), 1, 1
            )
            if k == CHUNKS - 1:
                codes_start, codes_wait, codes_finish = to_all(codes_buf, code_sem)
                codes_buf[me] = (own_codes * token_chosen).astype(BF16)
                codes_start()
            forward(k)

    maps[...] = map_reduce.result().astype(BF16)
    codes_wait()
    codes = jnp.sum(codes_buf[...].astype(F32), axis=0).astype(BF16)

    for b in range(blocks):
        tokens_b = slice(b * BLOCK, (b + 1) * BLOCK)
        codes_b = codes[:, tokens_b]
        live = lax.broadcasted_iota(jnp.int32, (BLOCK, 1), 0) < live_ref[b]

        def activate(t, b=b, tokens_b=tokens_b, codes_b=codes_b, live=live):
            span = pl.ds(pl.multiple_of(t * half, 128), half)
            map_b = maps[b * rank:(b + 1) * rank, span]
            gate = acc_g[tokens_b, span] + ADAPTER_SCALE * dot(codes_b, map_b, 0, 0)
            s = 1.0 / (1.0 + jnp.exp(-gate))
            grad = jnp.where(live, hid_ref[tokens_b, span].astype(F32), 0.0)
            grad_s = grad * s
            dgate[tokens_b, span] = (
                grad_s * acc_u[tokens_b, span] * (1.0 + gate * (1.0 - s))
            ).astype(BF16)
            dup[tokens_b, span] = (grad_s * gate).astype(BF16)

        each(0, hidden // half, activate)

    cgrad_start, cgrad_wait, cgrad_finish = to_all(cgrad_buf, cgrad_sem)
    for b in range(blocks):
        tokens_b = slice(b * BLOCK, (b + 1) * BLOCK)
        cgrad_buf[me, :, tokens_b] = dot(
            maps[b * rank:(b + 1) * rank, :], dgate[tokens_b, :], 1, 1
        )
    cgrad_start()
    for b in range(blocks):
        tokens_b = slice(b * BLOCK, (b + 1) * BLOCK)
        ugrad_buf[me, b * rank:(b + 1) * rank, :] = (
            ADAPTER_SCALE * dot(codes[:, tokens_b], dgate[tokens_b, :], 1, 0)
        ).astype(BF16)
    ugather = Gather(lambda shard: ugrad_buf.at[shard], uz_sem, uy_sem, uc_sem, 0)
    ugather.start()

    ct = 256 if cw % 256 == 0 else 128

    def backward(k):
        def step(t):
            cols = pl.ds(pl.multiple_of(k * cw + t * ct, 128), ct)
            value = dot(dgate[...], wg[:, cols], 1, 0) + dot(dup[...], wu[:, cols], 1, 0)
            part[k, :, :, pl.ds(pl.multiple_of(t * ct, 128), ct)] = value.reshape(n, rows, ct)

        each(0, cw // ct, step)

    def add_adapter(k, cg):
        def step(t):
            cols = pl.ds(pl.multiple_of(k * cw + t * ct, 128), ct)
            span = pl.ds(pl.multiple_of(t * ct, 128), ct)
            value = ADAPTER_SCALE * dot(cg, down_ref[:, cols], 0, 0)
            part[k, :, :, span] += value.reshape(n, rows, ct)

        each(0, cw // ct, step)

    reduces = [
        Reduce(
            lambda i, k=k: part[k, i],
            (cs_buf, cr_buf, ys_buf, yr_buf, zs_buf, zr_buf),
            (rc_sem, ry_sem, rz_sem),
            k,
        )
        for k in range(CHUNKS)
    ]

    def store(k):
        din_ref[:, k * cw:(k + 1) * cw] = reduces[k].result().astype(BF16)

    cg = None
    for i in range(CHUNKS):
        backward(i)
        if i == 0:
            cgrad_wait()
            cg = jnp.sum(cgrad_buf[...], axis=0).astype(BF16).astype(F32)
            cg = (cg * token_chosen).astype(BF16)
            ugather.on_z()
        if i == 1:
            ugather.on_y()
        add_adapter(i, cg)
        reduces[i].start()
        if i >= 1:
            reduces[i - 1].on_c()
        if i >= 2:
            reduces[i - 2].on_y()
        if i >= 3:
            store(i - 3)
    last = CHUNKS - 1
    reduces[last].on_c()
    if last >= 1:
        reduces[last - 1].on_y()

    for k in range(CHUNKS):
        ddown_ref[:, k * cw:(k + 1) * cw] = (
            ADAPTER_SCALE * dot(cg, token_chunk(k), 1, 0)
        ).astype(BF16)
    reduces[last].on_y()

    ugather.on_c()

    def put(d):
        value = jnp.zeros((rank, hidden), F32)
        for b in range(blocks):
            value = value + chosen[b] * ugrad_buf[d, b * rank:(b + 1) * rank, :].astype(F32)
        dmaps_ref[:, pl.ds(pl.multiple_of(d * hidden, 128), hidden)] = value.astype(BF16)

    each(0, n, put)
    for k in range(max(0, CHUNKS - 3), CHUNKS):
        store(k)
    for g in gathers:
        g.finish()
    ugather.finish()
    map_reduce.finish()
    codes_finish()
    cgrad_finish()
    for r in reduces:
        r.finish()


def body(
    nrow,
    ncol,
    tokens,
    hidden_gradient,
    gate_projection_weight,
    up_projection_weight,
    adapter_down_maps,
    adapter_up_maps,
    padded_block_tenant,
    tenant_adapter_slot,
    block_live_count,
):
    n = nrow * ncol
    ny = 2 if ncol == 1 else 1
    nz = n // (2 * ny)
    rows = tokens.shape[0] // ncol
    if ncol > 1:
        tokens = lax.dynamic_slice_in_dim(tokens, lax.axis_index("col") * rows, rows, 0)
    width = tokens.shape[1]
    total = n * rows
    hidden = gate_projection_weight.shape[0]
    rank = adapter_up_maps.shape[1]
    blocks = total // BLOCK
    cw = width // CHUNKS
    mr = blocks * rank
    half = nz * ny
    vmem = pl.BlockSpec(memory_space=pltpu.VMEM)
    smem = pl.BlockSpec(memory_space=pltpu.SMEM)
    hbm = pl.BlockSpec(memory_space=pl.ANY)
    sem = pltpu.SemaphoreType.DMA
    scratch = [
        pltpu.VMEM((hidden, width), BF16),
        pltpu.VMEM((hidden, width), BF16),
        pltpu.VMEM((n, rows, width), BF16),
        pltpu.VMEM((total, hidden), F32),
        pltpu.VMEM((total, hidden), F32),
        pltpu.VMEM((total, hidden), BF16),
        pltpu.VMEM((total, hidden), BF16),
        pltpu.VMEM((CHUNKS, n, rows, cw), F32),
        pltpu.VMEM((CHUNKS, half, rows, cw), BF16),
        pltpu.VMEM((CHUNKS, half, rows, cw), BF16),
        pltpu.VMEM((CHUNKS, nz, rows, cw), BF16),
        pltpu.VMEM((CHUNKS, nz, rows, cw), BF16),
        pltpu.VMEM((CHUNKS, nz, rows, cw), BF16),
        pltpu.VMEM((CHUNKS, nz, rows, cw), BF16),
        pltpu.VMEM((1, half, mr, hidden), BF16),
        pltpu.VMEM((1, half, mr, hidden), BF16),
        pltpu.VMEM((1, nz, mr, hidden), BF16),
        pltpu.VMEM((1, nz, mr, hidden), BF16),
        pltpu.VMEM((1, nz, mr, hidden), BF16),
        pltpu.VMEM((1, nz, mr, hidden), BF16),
        pltpu.VMEM((mr, hidden), BF16),
        pltpu.VMEM((n, rank, total), BF16),
        pltpu.VMEM((n, rank, total), F32),
        pltpu.VMEM((n, mr, hidden), BF16),
        sem((CHUNKS, 2)),
        sem((2, CHUNKS, nz)),
        sem((2, CHUNKS, nz)),
        sem((2, CHUNKS, half)),
        sem((2, 1, nz)),
        sem((2, 1, nz)),
        sem((2, 1, half)),
        sem((2, CHUNKS)),
        sem((2, CHUNKS)),
        sem((2, CHUNKS, nz)),
        sem((2, 1)),
        sem((2, 1)),
        sem((2, 1, nz)),
        sem((2, n)),
        sem((2, n)),
    ]
    input_gradient, down_t, up_grad = pl.pallas_call(
        functools.partial(kernel, (nz, ny, ncol)),
        out_shape=(
            jax.ShapeDtypeStruct((rows, width), BF16),
            jax.ShapeDtypeStruct((rank, width), BF16),
            jax.ShapeDtypeStruct((rank, n * hidden), BF16),
        ),
        in_specs=[vmem, vmem, hbm, hbm, vmem, vmem, smem, smem, smem],
        out_specs=(vmem, vmem, vmem),
        scratch_shapes=scratch,
        compiler_params=pltpu.CompilerParams(
            collective_id=0, has_side_effects=True, vmem_limit_bytes=62 * 1024 * 1024
        ),
    )(
        tokens,
        hidden_gradient,
        gate_projection_weight,
        up_projection_weight,
        jnp.swapaxes(adapter_down_maps[0], 0, 1),
        adapter_up_maps[0],
        padded_block_tenant,
        tenant_adapter_slot,
        block_live_count,
    )
    return input_gradient, jnp.swapaxes(down_t, 0, 1)[None], up_grad[None]


def solution(mesh):
    return jax.shard_map(
        functools.partial(body, mesh.shape["row"], mesh.shape["col"]),
        mesh=mesh,
        in_specs=(
            P(("groups", "row"), None),
            P("groups", ("row", "col")),
            P(("row", "col"), None),
            P(("row", "col"), None),
            P(("groups", "row", "col"), None, None),
            P(("groups", "row", "col"), None, None),
            P("groups"),
            P("groups"),
            P("groups"),
        ),
        out_specs=(
            P(("groups", "row", "col"), None),
            P(("groups", "row", "col"), None, None),
            P(("groups", "row", "col"), None, None),
        ),
        check_vma=False,
    )
```

time: 497 us -> 107 us (0.22)
  other arithmetic: 137 us -> 0 us
  blocking collectives: 119 us -> 0 us
  Pallas kernels: 0 us -> 100 us
  matrix products: 89.1 us -> 0 us
  local copies, waits for them, and re-layouts: 86.8 us -> 5.25 us
  waiting for transfers between devices: 35.4 us -> 0 us
  between operations: 14.2 us -> 0.64 us
  starting transfers between devices: 11.3 us -> 0 us
    unnamed x1 -> x0, other arithmetic: 135 us -> none
    psum x2 -> x0, blocking collectives: 119 us -> none  [the longest x1 61.5 us: body(): latent_rows = lax.psum(code_part, ('row', 'col')).astype(jnp.bfloat16)]
    pallas_call x0 -> x1, Pallas kernels: none -> 100 us  [body(): pl.pallas_call(functools.partial(kernel, (nz, ny, ncol)), out_shape=(jax....]
    dot_general x13 -> x0, matrix products: 89.1 us -> none  [the longest x1 35.5 us: body(): jnp.einsum('bs,bdr->sdr', local_selection.astype(jnp.float32), blockwise_...]
    unnamed x19 -> x3, local copies, waits for them, and re-layouts: 45.8 us -> 5.25 us
    all_to_all x2 -> x0, local copies, waits for them, and re-layouts: 23.5 us -> none  [the longest x1 22.6 us: body(): lax.all_to_all(adapter_up_maps, ('row', 'col'), split_axis=2, concat_axis...]
    all_to_all x2 -> x0, waiting for transfers between devices: 18.3 us -> none  [the longest x1 18.3 us: body(): lax.all_to_all(adapter_up_maps, ('row', 'col'), split_axis=2, concat_axis...]
    reduce_scatter x1 -> x0, waiting for transfers between devices: 16.3 us -> none  [body(): lax.psum_scatter(primary_rows + adapter_input_term, ('row', 'col'), scatt...]
  transfers between devices with their start and end apart: 4 -> 0, of which waited for: 2 -> 0; matrix products, arithmetic and copies ran while one was open for 53% -> 0% of each run, Pallas kernels for 0% -> 0%
where the time goes in v1:
time: 107 us; the launch traced here: 106 us
  Pallas kernels  100 us (93%)
  local copies, waits for them, and re-layouts  5.25 us (5%)
    pallas_call x1, Pallas kernels, body(): pl.pallas_call(functools.partial(kernel, (nz, ny, ncol)), out_shape=(jax....  100 us
    unnamed x3, local copies, waits for them, and re-layouts  5.25 us

profile of v1, /device:TPU:0, one launch (start us, length us, event | category | flops | bytes accessed | tf_op | source)
XLA Modules:
  0.0 106.3 jit_solution(6973564752972917515)
XLA Ops:
  0.6 100.4 %shard_map.112 = (bf16[16,5120]{1,0:T(8,128)(2,1)}, bf16[16,5120]{1,0:T(8,128)(2,1)}, bf16[16,24576]{1,0:T(8,128)(2,1)}) custom-call(bf16[16,5120]{1,0:T(8,128)(2,1)} %tok_in.1, bf16[256,1536]{1,0:T(8,128)(2,1)} %hid_ref.1, bf16[1536,5120]{1,0:T(8,128)(2,1)} %gate_hbm.1, bf16[1536,5120]{1,0:T(8,128)(2,1)} %up_hbm.1, bf16[16,5120]{1,0:T(8,128)(2,1)} %bitcast.11, ...), custom_call_target="tpu_custom_call" | custom-call | tf_op jit(solution)/shard_map/pallas_call | solution.py:482
  101.1 1.6 %copy.15 = bf16[16,5120]{1,0:T(8,128)(2,1)} copy(bf16[16,5120]{1,0:T(8,128)(2,1)} %get-tuple-element.12) | data formatting | bytes 327680
  102.6 1.6 %copy.16 = bf16[1,5120,16]{1,2,0:T(8,128)(2,1)} copy(bf16[1,5120,16]{1,2,0:T(8,128)(2,1)} %bitcast.10) | data formatting | bytes 327680
  104.2 2.1 %copy.17 = bf16[1,16,24576]{2,1,0:T(8,128)(2,1)} copy(bf16[1,16,24576]{2,1,0:T(8,128)(2,1)} %bitcast.8) | data formatting | bytes 1572864

commit v2 on v1

--- a/solution.py
+++ b/solution.py
@@ -202,15 +202,45 @@
                 self.y_copy.wait_send()
             each(1, nz, lambda d: self.z_copy(d).wait_send())
 
-    def to_all(buf, sem):
-        def copy(d, shard):
-            return remote(buf.at[shard], buf.at[shard], (sem.at[0, d], sem.at[1, d]), (me + d) % n)
-
-        return (
-            lambda: each(1, n, lambda d: copy(d, me).start()),
-            lambda: each(1, n, lambda d: copy(d, (me + n - d) % n).wait_recv()),
-            lambda: each(1, n, lambda d: copy(d, me).wait_send()),
-        )
+    class Sum:
+        def __init__(self, buf, sem):
+            self.buf, self.sem = buf, sem
+
+        def pair(self, i, target):
+            sems = (self.sem.at[0, i], self.sem.at[1, i])
+            return remote(self.buf.at[2 * i], self.buf.at[2 * i + 1], sems, target)
+
+        def z_copy(self, d):
+            sems = (self.sem.at[0, 1 + d], self.sem.at[1, 1 + d])
+            return remote(self.buf.at[4], self.buf.at[4 + d], sems, index((z + d) % nz, y, c))
+
+        def start(self):
+            self.pair(0, c_peer).start()
+
+        def on_c(self):
+            self.pair(0, c_peer).wait_recv()
+            value = self.buf[0].astype(F32) + self.buf[1].astype(F32)
+            self.buf[2] = value.astype(self.buf.dtype)
+            if ny > 1:
+                self.pair(1, y_peer).start()
+
+        def on_y(self):
+            value = self.buf[2].astype(F32)
+            if ny > 1:
+                self.pair(1, y_peer).wait_recv()
+                value = value + self.buf[3].astype(F32)
+            self.buf[4] = value.astype(self.buf.dtype)
+            each(1, nz, lambda d: self.z_copy(d).start())
+
+        def result(self):
+            each(1, nz, lambda d: self.z_copy(d).wait_recv())
+            return jnp.sum(self.buf[4:4 + nz].astype(F32), axis=0).astype(BF16)
+
+        def finish(self):
+            self.pair(0, c_peer).wait_send()
+            if ny > 1:
+                self.pair(1, y_peer).wait_send()
+            each(1, nz, lambda d: self.z_copy(d).wait_send())
 
     slots = [slot_ref[tenant_ref[b]] for b in range(blocks)]
     chosen = [jnp.where(s == me, 1.0, 0.0).astype(F32) for s in slots]
@@ -269,12 +299,10 @@
     for i in range(CHUNKS + 2):
         if i < CHUNKS:
             gathers[i].on_z()
-        if i == CHUNKS - 1:
+        if i == 0:
             map_reduce.on_c()
         if 0 <= i - 1 < CHUNKS:
             gathers[i - 1].on_y()
-        if i == CHUNKS:
-            map_reduce.on_y()
         if i >= 2:
             k = i - 2
             gathers[k].on_c()
@@ -282,14 +310,17 @@
                 down_ref[:, k * cw:(k + 1) * cw], token_chunk(k), 1, 1
             )
             if k == CHUNKS - 1:
-                codes_start, codes_wait, codes_finish = to_all(codes_buf, code_sem)
-                codes_buf[me] = (own_codes * token_chosen).astype(BF16)
-                codes_start()
+                code_sum = Sum(codes_buf, code_sem)
+                codes_buf[0] = (own_codes * token_chosen).astype(BF16)
+                code_sum.start()
+                code_sum.on_c()
             forward(k)
-
+            if k == min(1, CHUNKS - 1):
+                map_reduce.on_y()
+
+    code_sum.on_y()
     maps[...] = map_reduce.result().astype(BF16)
-    codes_wait()
-    codes = jnp.sum(codes_buf[...].astype(F32), axis=0).astype(BF16)
+    codes = code_sum.result()
 
     for b in range(blocks):
         tokens_b = slice(b * BLOCK, (b + 1) * BLOCK)
@@ -310,13 +341,13 @@
 
         each(0, hidden // half, activate)
 
-    cgrad_start, cgrad_wait, cgrad_finish = to_all(cgrad_buf, cgrad_sem)
+    cgrad_sum = Sum(cgrad_buf, cgrad_sem)
     for b in range(blocks):
         tokens_b = slice(b * BLOCK, (b + 1) * BLOCK)
-        cgrad_buf[me, :, tokens_b] = dot(
+        cgrad_buf[0, :, tokens_b] = dot(
             maps[b * rank:(b + 1) * rank, :], dgate[tokens_b, :], 1, 1
         )
-    cgrad_start()
+    cgrad_sum.start()
     for b in range(blocks):
         tokens_b = slice(b * BLOCK, (b + 1) * BLOCK)
         ugrad_buf[me, b * rank:(b + 1) * rank, :] = (
@@ -324,6 +355,7 @@
         ).astype(BF16)
     ugather = Gather(lambda shard: ugrad_buf.at[shard], uz_sem, uy_sem, uc_sem, 0)
     ugather.start()
+    cgrad_sum.on_c()
 
     ct = 256 if cw % 256 == 0 else 128
 
@@ -357,18 +389,20 @@
     def store(k):
         din_ref[:, k * cw:(k + 1) * cw] = reduces[k].result().astype(BF16)
 
-    cg = None
+    backward(0)
+    cgrad_sum.on_y()
+    ugather.on_z()
+    if CHUNKS > 1:
+        backward(1)
+    cg = cgrad_sum.result().astype(F32)
+    cg = (cg * token_chosen).astype(BF16)
     for i in range(CHUNKS):
-        backward(i)
-        if i == 0:
-            cgrad_wait()
-            cg = jnp.sum(cgrad_buf[...], axis=0).astype(BF16).astype(F32)
-            cg = (cg * token_chosen).astype(BF16)
-            ugather.on_z()
+        if i >= 2:
+            backward(i)
+        add_adapter(i, cg)
+        reduces[i].start()
         if i == 1:
             ugather.on_y()
-        add_adapter(i, cg)
-        reduces[i].start()
         if i >= 1:
             reduces[i - 1].on_c()
         if i >= 2:
@@ -401,8 +435,8 @@
         g.finish()
     ugather.finish()
     map_reduce.finish()
-    codes_finish()
-    cgrad_finish()
+    code_sum.finish()
+    cgrad_sum.finish()
     for r in reduces:
         r.finish()
 
@@ -460,8 +494,8 @@
         pltpu.VMEM((1, nz, mr, hidden), BF16),
         pltpu.VMEM((1, nz, mr, hidden), BF16),
         pltpu.VMEM((mr, hidden), BF16),
-        pltpu.VMEM((n, rank, total), BF16),
-        pltpu.VMEM((n, rank, total), F32),
+        pltpu.VMEM((4 + nz, rank, total), BF16),
+        pltpu.VMEM((4 + nz, rank, total), F32),
         pltpu.VMEM((n, mr, hidden), BF16),
         sem((CHUNKS, 2)),
         sem((2, CHUNKS, nz)),
@@ -476,8 +510,8 @@
         sem((2, 1)),
         sem((2, 1)),
         sem((2, 1, nz)),
-        sem((2, n)),
-        sem((2, n)),
+        sem((2, 1 + nz)),
+        sem((2, 1 + nz)),
     ]
     input_gradient, down_t, up_grad = pl.pallas_call(
         functools.partial(kernel, (nz, ny, ncol)),

time: 107 us -> 97.9 us (0.915)
  Pallas kernels: 100 us -> 91.8 us
    pallas_call x1, Pallas kernels: 100 us -> 91.8 us  [body(): pl.pallas_call(functools.partial(kernel, (nz, ny, ncol)), out_shape=(jax....]
where the time goes in v2:
time: 97.9 us; the launch traced here: 97.7 us
  Pallas kernels  91.8 us (94%)
  local copies, waits for them, and re-layouts  5.25 us (5%)
    pallas_call x1, Pallas kernels, body(): pl.pallas_call(functools.partial(kernel, (nz, ny, ncol)), out_shape=(jax....  91.8 us
    unnamed x3, local copies, waits for them, and re-layouts  5.25 us

profile of v2, /device:TPU:0, one launch (start us, length us, event | category | flops | bytes accessed | tf_op | source)
XLA Modules:
  0.0 97.7 jit_solution(14612907543821539795)
XLA Ops:
  0.6 91.8 %shard_map.112 = (bf16[16,5120]{1,0:T(8,128)(2,1)}, bf16[16,5120]{1,0:T(8,128)(2,1)}, bf16[16,24576]{1,0:T(8,128)(2,1)}) custom-call(bf16[16,5120]{1,0:T(8,128)(2,1)} %tok_in.1, bf16[256,1536]{1,0:T(8,128)(2,1)} %hid_ref.1, bf16[1536,5120]{1,0:T(8,128)(2,1)} %gate_hbm.1, bf16[1536,5120]{1,0:T(8,128)(2,1)} %up_hbm.1, bf16[16,5120]{1,0:T(8,128)(2,1)} %bitcast.11, ...), custom_call_target="tpu_custom_call" | custom-call | tf_op jit(solution)/shard_map/pallas_call | solution.py:516
  92.4 1.6 %copy.15 = bf16[16,5120]{1,0:T(8,128)(2,1)} copy(bf16[16,5120]{1,0:T(8,128)(2,1)} %get-tuple-element.12) | data formatting | bytes 327680
  94.0 1.6 %copy.16 = bf16[1,5120,16]{1,2,0:T(8,128)(2,1)} copy(bf16[1,5120,16]{1,2,0:T(8,128)(2,1)} %bitcast.10) | data formatting | bytes 327680
  95.6 2.1 %copy.17 = bf16[1,16,24576]{2,1,0:T(8,128)(2,1)} copy(bf16[1,16,24576]{2,1,0:T(8,128)(2,1)} %bitcast.8) | data formatting | bytes 1572864

commit v3 on v2

--- a/solution.py
+++ b/solution.py
@@ -277,7 +277,7 @@
     def token_chunk(k):
         return tok[:, :, k * cw:(k + 1) * cw].reshape(total, cw)
 
-    def forward(k):
+    def forward(k, between=()):
         weight_copy(k, 0).wait()
         weight_copy(k, 1).wait()
         tk = token_chunk(k)
@@ -293,7 +293,14 @@
                 acc_g[:, span] += g
                 acc_u[:, span] += u
 
-        each(0, hidden // tile, step)
+        tiles = hidden // tile
+        at = 0
+        for action in between:
+            if at < tiles:
+                each(at, at + 1, step)
+                at += 1
+            action()
+        each(at, tiles, step)
 
     own_codes = jnp.zeros((rank, total), F32)
     for i in range(CHUNKS + 2):
@@ -313,12 +320,12 @@
                 code_sum = Sum(codes_buf, code_sem)
                 codes_buf[0] = (own_codes * token_chosen).astype(BF16)
                 code_sum.start()
-                code_sum.on_c()
-            forward(k)
+                forward(k, (code_sum.on_c, code_sum.on_y))
+            else:
+                forward(k)
             if k == min(1, CHUNKS - 1):
                 map_reduce.on_y()
 
-    code_sum.on_y()
     maps[...] = map_reduce.result().astype(BF16)
     codes = code_sum.result()
 

time: 97.9 us -> 97.1 us (level)
  no operation moved by 1% of the time
where the time goes in v3:
time: 97.1 us; the launch traced here: 96.9 us
  Pallas kernels  91 us (94%)
  local copies, waits for them, and re-layouts  5.25 us (5%)
    pallas_call x1, Pallas kernels, body(): pl.pallas_call(functools.partial(kernel, (nz, ny, ncol)), out_shape=(jax....  91 us
    unnamed x3, local copies, waits for them, and re-layouts  5.25 us

profile of v3, /device:TPU:0, one launch (start us, length us, event | category | flops | bytes accessed | tf_op | source)
XLA Modules:
  0.0 96.9 jit_solution(215405469264812375)
XLA Ops:
  0.6 91.0 %shard_map.112 = (bf16[16,5120]{1,0:T(8,128)(2,1)}, bf16[16,5120]{1,0:T(8,128)(2,1)}, bf16[16,24576]{1,0:T(8,128)(2,1)}) custom-call(bf16[16,5120]{1,0:T(8,128)(2,1)} %tok_in.1, bf16[256,1536]{1,0:T(8,128)(2,1)} %hid_ref.1, bf16[1536,5120]{1,0:T(8,128)(2,1)} %gate_hbm.1, bf16[1536,5120]{1,0:T(8,128)(2,1)} %up_hbm.1, bf16[16,5120]{1,0:T(8,128)(2,1)} %bitcast.11, ...), custom_call_target="tpu_custom_call" | custom-call | tf_op jit(solution)/shard_map/pallas_call | solution.py:523
  91.7 1.6 %copy.15 = bf16[16,5120]{1,0:T(8,128)(2,1)} copy(bf16[16,5120]{1,0:T(8,128)(2,1)} %get-tuple-element.12) | data formatting | bytes 327680
  93.3 1.6 %copy.16 = bf16[1,5120,16]{1,2,0:T(8,128)(2,1)} copy(bf16[1,5120,16]{1,2,0:T(8,128)(2,1)} %bitcast.10) | data formatting | bytes 327680
  94.8 2.1 %copy.17 = bf16[1,16,24576]{2,1,0:T(8,128)(2,1)} copy(bf16[1,16,24576]{2,1,0:T(8,128)(2,1)} %bitcast.8) | data formatting | bytes 1572864
